TPU v7x, 256 devices: a whole 4x4x8 slice. The times are simulated.
256 devices in a mesh: ctx: 32 (over z, x), head: 8 (over y, core).
Axes of the slice: x: 4, y: 4, z: 8, core: 2. Of those that a mesh axis runs over, the one named last changes fastest.
Arguments:
- tokens: bfloat16 [4096, 2048], P('ctx'), may hold values from -6 to 6
- doc_lengths: int32 [16], replicated, may hold values from 1 to 2048, 4096 in all
- w_query: bfloat16 [2048, 2048], P(None, 'head'), may hold values from -0.125 to 0.125
- w_key: bfloat16 [2048, 2048], P(None, 'head'), may hold values from -0.125 to 0.125
- w_value: bfloat16 [2048, 4096], P(None, 'head'), may hold values from -0.125 to 0.125
- w_gate: bfloat16 [2048, 4096], P(None, 'head'), may hold values from -0.125 to 0.125
- conv_query: bfloat16 [4, 2048], P(None, 'head'), may hold values from -3 to 3
- conv_key: bfloat16 [4, 2048], P(None, 'head'), may hold values from -3 to 3
- conv_value: bfloat16 [4, 4096], P(None, 'head'), may hold values from -3 to 3
- beta_logit: float32 [32, 4096], P('head', 'ctx'), may hold values from -6 to 6
- decay_logit: float32 [32, 4096], P('head', 'ctx'), may hold values from -3 to 4096
- a_log: float32 [32], P('head')
- w_output: bfloat16 [4096, 2048], P('head'), may hold values from -0.09375 to 0.09375
Outputs:
- mixed: bfloat16 [4096, 2048], P(('ctx', 'head'))
Inputs may be any that keep to these rules, and one draw needn't show every extreme that they name: `doc_lengths`: lengths of the documents in packing order; they sum to 4096, and the longest has exactly 2048 tokens.
All inputs are finite; a program needn't handle non-finite values.
Results may differ from a plain program's by a relative error of at most 0.023.
Values may be sent and summed in bfloat16 or wider, within the bound.
A program may use at most 128 MiB of HBM per device.

v0:
```python
import jax
import jax.numpy as jnp
from jax import lax
from jax.sharding import PartitionSpec as P

DK = 128
DV = 128
STRETCH = 64


HIGHP = lax.Precision.HIGHEST


def entering(value, axis, join, neutral):
    count, mine = (lax.axis_size(axis), lax.axis_index(axis))
    pieces = jax.tree.map(lambda part: lax.all_gather(part, axis), value)
    subtotal = jax.tree.map(
        lambda part, zero: jnp.full_like(part, 0) + jnp.asarray(zero, part.dtype), value, neutral
    )

    def step(position, subtotal):
        longer = join(subtotal, jax.tree.map(lambda part: part[position], pieces))
        return jax.tree.map(lambda new, old: jnp.where(position < mine, new, old), longer, subtotal)

    return lax.fori_loop(0, count - 1, step, subtotal)


def shifted(block, axis, distance):
    devices = range(lax.axis_size(axis))
    route = [(i - distance, i) for i in devices if i - distance in devices]
    return lax.ppermute(block, axis, route)


def batched_heads(form, left_op, right_op):
    return jnp.einsum(form, left_op, right_op, precision=HIGHP)


def doc_tables(doc_lengths, positions):
    doc_ends = jnp.cumsum(doc_lengths)
    offsets = doc_ends - doc_lengths
    starts = jnp.any(positions[:, None] == offsets[None, :], axis=1)
    doc_ids = jnp.sum((offsets[None, 1:] <= positions[:, None]).astype(jnp.int32), axis=1)
    return (starts, doc_ids)


def short_conv(extended, weight, positions, doc_ids):
    tap_count = weight.shape[0]
    row_count = extended.shape[0] - tap_count + 1
    here_docs = doc_ids[tap_count - 1 :]
    running_sum = jnp.zeros((row_count, extended.shape[1]), jnp.float32)
    for tap_index in range(tap_count):
        window = extended[tap_index : tap_index + row_count].astype(jnp.float32)
        keep_rows = (doc_ids[tap_index : tap_index + row_count] == here_docs) & (
            positions[tap_index : tap_index + row_count] >= 0
        )
        running_sum = running_sum + jnp.where(
            keep_rows[:, None], weight[tap_index].astype(jnp.float32)[None, :] * window, 0.0
        )
    return jax.nn.silu(running_sum)


def unit_norm(field):
    return field * lax.rsqrt(jnp.sum(field * field, axis=-1, keepdims=True) + 1e-06)


def stretch_parts(
    query_matrix_rows, key_matrix_rows, value_rows, beta_rate, log_decay, doc_ids, prev_doc
):
    span_len = query_matrix_rows.shape[1]
    index_line = jnp.arange(span_len, dtype=jnp.int32)
    lower_incl = index_line[:, None] >= index_line[None, :]
    tri_ones = lower_incl.astype(jnp.float32)
    cumulative = batched_heads("ij,hj->hi", tri_ones, log_decay)
    same_doc = (doc_ids[:, None] == doc_ids[None, :]) & lower_incl
    decay_gap = jnp.where(same_doc[None], cumulative[:, :, None] - cumulative[:, None, :], 0.0)
    decay_mat = jnp.where(same_doc[None], jnp.exp(decay_gap), 0.0)
    kept_flag = (doc_ids == prev_doc).astype(jnp.float32)
    per_head_decay = jnp.exp(cumulative) * kept_flag[None, :]
    key_gram = batched_heads("hik,hjk->hij", key_matrix_rows, key_matrix_rows)
    strict_low = index_line[:, None] > index_line[None, :]
    lower_part = jnp.where(strict_low[None], beta_rate[:, :, None] * decay_mat * key_gram, 0.0)
    system = lower_part + jnp.eye(span_len, dtype=jnp.float32)[None]
    right_side = jnp.concatenate(
        [
            beta_rate[:, :, None] * value_rows,
            (beta_rate * per_head_decay)[:, :, None] * key_matrix_rows,
        ],
        axis=2,
    )
    solved = jax.scipy.linalg.solve_triangular(system, right_side, lower=True, unit_diagonal=True)
    value_width = value_rows.shape[2]
    state_update = solved[:, :, :value_width]
    weighted_values = solved[:, :, value_width:]
    attention_scores = decay_mat * batched_heads("hik,hjk->hij", query_matrix_rows, key_matrix_rows)
    final_row = decay_mat[:, span_len - 1, :]
    return (per_head_decay, state_update, weighted_values, attention_scores, final_row)


def stretch_out(stretch_terms, entry_state, query_matrix_rows, key_matrix_rows):
    per_head_decay, state_update, weighted_values, attention_scores, final_row = stretch_terms
    corrected_values = state_update - batched_heads("xyz,xzr->xyr", weighted_values, entry_state)
    segment_output = per_head_decay[:, :, None] * batched_heads(
        "xyz,xzr->xyr", query_matrix_rows, entry_state
    ) + batched_heads("uyc,ucb->uyb", attention_scores, corrected_values)
    updated_state = per_head_decay[:, -1][:, None, None] * entry_state + batched_heads(
        "uyf,uyz->ufz", final_row[:, :, None] * key_matrix_rows, corrected_values
    )
    return (segment_output, updated_state)


def transition(stretch_terms, key_matrix_rows):
    per_head_decay, state_update, weighted_values, attention_scores, final_row = stretch_terms
    key_scaled_rows = final_row[:, :, None] * key_matrix_rows
    key_width = key_matrix_rows.shape[2]
    eye_block = jnp.eye(key_width, dtype=jnp.float32)[None]
    step_trans = per_head_decay[:, -1][:, None, None] * eye_block - batched_heads(
        "hck,hcl->hkl", key_scaled_rows, weighted_values
    )
    stepwise_state = batched_heads("uyf,uyz->ufz", key_scaled_rows, state_update)
    return (step_trans, stepwise_state)


def blocks_three(field, stretch_count, stretch_len):
    return jnp.transpose(
        field.reshape(field.shape[0], stretch_count, stretch_len, field.shape[2]), (1, 0, 2, 3)
    )


def blocks_two(field, stretch_count, stretch_len):
    return jnp.transpose(field.reshape(field.shape[0], stretch_count, stretch_len), (1, 0, 2))


def compose(after_pair, before_pair):
    return (
        batched_heads("hij,hjk->hik", after_pair[0], before_pair[0]),
        batched_heads("hij,hjk->hik", after_pair[0], before_pair[1]) + after_pair[1],
    )


def pass_states(trans_prod, local_state):

    def combine(earlier, later_pair):
        return compose(later_pair, earlier)

    identity_pair = (
        jnp.broadcast_to(jnp.eye(trans_prod.shape[1], dtype=jnp.float32), trans_prod.shape),
        jnp.zeros_like(local_state),
    )
    prefix = entering((trans_prod, local_state), "ctx", combine, identity_pair)
    incoming = prefix[1]
    return incoming


def per_device(
    tokens,
    doc_lengths,
    w_query,
    w_key,
    w_value,
    w_gate,
    conv_query,
    conv_key,
    conv_value,
    beta_logit,
    decay_logit,
    a_log,
    w_output,
):
    row_count = tokens.shape[0]
    conv_lag = conv_query.shape[0] - 1
    key_cols = w_query.shape[1]
    value_cols = w_value.shape[1]
    key_group = key_cols // DK
    value_group = value_cols // DV
    ratio_heads = value_group // key_group
    stretch_count = row_count // STRETCH
    proj_query = jnp.dot(tokens, w_query, preferred_element_type=jnp.float32).astype(jnp.bfloat16)
    proj_key = jnp.dot(tokens, w_key, preferred_element_type=jnp.float32).astype(jnp.bfloat16)
    proj_value = jnp.dot(tokens, w_value, preferred_element_type=jnp.float32).astype(jnp.bfloat16)
    proj_gate = jnp.dot(tokens, w_gate, preferred_element_type=jnp.float32).astype(jnp.bfloat16)
    halo_rows = shifted(
        (
            proj_query[row_count - conv_lag :],
            proj_key[row_count - conv_lag :],
            proj_value[row_count - conv_lag :],
        ),
        "ctx",
        1,
    )
    block_first = lax.axis_index("ctx") * row_count
    positions = block_first + jnp.arange(-conv_lag, row_count, dtype=jnp.int32)
    starts, doc_ids = doc_tables(doc_lengths, positions)
    own_docs = doc_ids[conv_lag:]
    own_starts = starts[conv_lag:].astype(jnp.int32)
    stretch_docs = own_docs.reshape(stretch_count, STRETCH)
    prev_docs = stretch_docs[:, 0] - own_starts.reshape(stretch_count, STRETCH)[:, 0]
    conv_q = short_conv(
        jnp.concatenate([halo_rows[0], proj_query], 0), conv_query, positions, doc_ids
    )
    conv_k = short_conv(jnp.concatenate([halo_rows[1], proj_key], 0), conv_key, positions, doc_ids)
    conv_v = short_conv(
        jnp.concatenate([halo_rows[2], proj_value], 0), conv_value, positions, doc_ids
    )
    query_heads = unit_norm(conv_q.reshape(row_count, key_group, DK)) * DK ** (-0.5)
    key_heads = unit_norm(conv_k.reshape(row_count, key_group, DK))
    query_heads = jnp.repeat(jnp.transpose(query_heads, (1, 0, 2)), ratio_heads, axis=0)
    key_heads = jnp.repeat(jnp.transpose(key_heads, (1, 0, 2)), ratio_heads, axis=0)
    value_heads = jnp.transpose(conv_v.reshape(row_count, value_group, DV), (1, 0, 2))
    beta_rate = jax.nn.sigmoid(beta_logit)
    log_decay = -jnp.exp(a_log)[:, None] * jax.nn.softplus(decay_logit)
    stretch_inputs = (
        blocks_three(query_heads, stretch_count, STRETCH),
        blocks_three(key_heads, stretch_count, STRETCH),
        blocks_three(value_heads, stretch_count, STRETCH),
        blocks_two(beta_rate, stretch_count, STRETCH),
        blocks_two(log_decay, stretch_count, STRETCH),
        stretch_docs,
        prev_docs,
    )
    identity_mat = jnp.broadcast_to(jnp.eye(DK, dtype=jnp.float32), (value_group, DK, DK))
    zero_state = jnp.zeros((value_group, DK, DV), jnp.float32)

    def terms_of(inputs):
        (
            query_matrix_rows,
            key_matrix_rows,
            value_rows,
            beta_rows,
            decay_rows,
            docs_here,
            prev_here,
        ) = inputs
        return (
            stretch_parts(
                query_matrix_rows,
                key_matrix_rows,
                value_rows,
                beta_rows,
                decay_rows,
                docs_here,
                prev_here,
            ),
            query_matrix_rows,
            key_matrix_rows,
        )

    def summarize(carried, inputs):
        stretch_terms, query_matrix_rows, key_matrix_rows = terms_of(inputs)
        step_pair = transition(stretch_terms, key_matrix_rows)
        return (compose(step_pair, carried), None)

    (trans_prod, local_state), _ = lax.scan(summarize, (identity_mat, zero_state), stretch_inputs)
    incoming = pass_states(trans_prod, local_state)

    def emit(entry_state, inputs):
        stretch_terms, query_matrix_rows, key_matrix_rows = terms_of(inputs)
        segment_output, updated_state = stretch_out(
            stretch_terms, entry_state, query_matrix_rows, key_matrix_rows
        )
        return (updated_state, segment_output)

    _, outputs = lax.scan(emit, incoming, stretch_inputs)
    outputs = jnp.transpose(outputs, (0, 2, 1, 3)).reshape(row_count, value_group, DV)
    gate_heads = proj_gate.reshape(row_count, value_group, DV).astype(jnp.float32)
    normed = outputs * lax.rsqrt(jnp.mean(outputs * outputs, axis=-1, keepdims=True) + 1e-06)
    gated_rows = (
        (normed * jax.nn.silu(gate_heads)).astype(jnp.bfloat16).reshape(row_count, value_cols)
    )
    summed = lax.psum_scatter(
        jnp.dot(gated_rows, w_output, preferred_element_type=jnp.float32).astype(jnp.bfloat16),
        "head",
        scatter_dimension=0,
        tiled=True,
    )
    return summed


def solution(mesh):
    in_specs = (
        P("ctx", None),
        P(),
        P(None, "head"),
        P(None, "head"),
        P(None, "head"),
        P(None, "head"),
        P(None, "head"),
        P(None, "head"),
        P(None, "head"),
        P("head", "ctx"),
        P("head", "ctx"),
        P("head"),
        P("head", None),
    )
    out_specs = P(("ctx", "head"), None)
    return jax.shard_map(
        per_device, mesh=mesh, in_specs=in_specs, out_specs=out_specs, check_vma=False
    )
```

profile of v0, /device:TPU:193, one launch (start us, length us, event | category | flops | bytes accessed | tf_op | source)
XLA Modules:
  0.0 424.2 jit_solution(1126550014325111702)
XLA Ops:
  6.6 1.8 convolution_convert_fusion.4
  8.5 3.1 collective-permute-start
  11.6 2.2 convolution_convert_fusion.2
  13.8 3.1 collective-permute-start.1
  18.6 1.3 fusion.96
  22.4 58.3 %while.40 = (s32[]{:T(128)}, f32[4,128,128]{2,1,0:T(8,128)S(1)}, f32[4,128,128]{2,1,0:T(8,128)}, f32[2,4,64]{2,1,0:T(4,128)}, s32[2,64]{1,0:T(2,128)}, /*index=5...) while((s32[]{:T(128)}, f32[4,128,128]{2,1,0:T(8,128)S(1)}, ...), condition=%wide.region_5.7_spmd.clone, body=%wide.region_4.6_spmd.clone.sunk | while | flops 378413760 | bytes 5081283 | solution.py:252
  22.4 1.2 dynamic_slice.165
  23.6 1.3 fusion.199
  27.6 19.7 %custom-call.12 = f32[4,1,64,64]{2,3,1,0:T(8,128)S(1)} custom-call(f32[4,1,64,64]{3,2,1,0:T(8,128)S(1)} %fusion.205), custom_call_target="InvertDiagBlocksLowerTriangular" | custom-call | tf_op jit(solution)/shard_map/while/body/eval_jaxpr/jit(_solve_triangular)/vmap()/triangular_solve | solution.py:90
  49.3 1.4 convolution_add_fusion.6
  51.1 1.2 dynamic_slice.165
  52.3 1.3 fusion.199
  56.3 19.7 %custom-call.12 = f32[4,1,64,64]{2,3,1,0:T(8,128)S(1)} custom-call(f32[4,1,64,64]{3,2,1,0:T(8,128)S(1)} %fusion.205), custom_call_target="InvertDiagBlocksLowerTriangular" | custom-call | tf_op jit(solution)/shard_map/while/body/eval_jaxpr/jit(_solve_triangular)/vmap()/triangular_solve | solution.py:90
  77.5 1.3 fusion.209
  78.9 1.4 convolution_add_fusion.6
  82.2 1.7 convolution_convert_fusion.3
  84.0 2.8 collective-permute-start.2
  86.8 3.6 collective-permute-done.2
  91.1 87.0 %all-gather.5.cloned.1.call-done = f32[128,128,128]{2,1,0:T(8,128)} async-done(((f32[4,128,128]{2,1,0:T(8,128)}), f32[128,128,128]{2,1,0:T(8,128)}) %all-gather.5.cloned.1.call-update) | async-done | bytes 8388624 | tf_op jit(solution)/shard_map/all_gather | solution.py:16
  178.1 98.0 %all-gather.7.cloned.1.call-done = f32[128,128,128]{2,1,0:T(8,128)} async-done(((f32[4,128,128]{2,1,0:T(8,128)}), f32[128,128,128]{2,1,0:T(8,128)}) %all-gather.7.cloned.1.call-update) | async-done | bytes 8388624 | tf_op jit(solution)/shard_map/all_gather | solution.py:16
  276.1 46.0 %while.41 = (s32[]{:T(128)}, f32[4,128,128]{2,1,0:T(8,128)S(1)}, s32[]{:T(128)}, f32[32,4,128,128]{3,2,1,0:T(8,128)}, f32[32,4,128,128]{3,2,1,0:T(8,128)}, /*index=5*/s32[]{:T(128)}, s32[]{:T(128)}) while((s32[]{:T(128)}, f32[4,128,128]{2,1,0:T(8,128)S(1)}, s32[]{:T(128)}, f32[32,4,128,128]{3,2,1,0:T(8,128)}, ...), condition=%wide.region_7.9_spmd.clone, body=%wide.region_6.8_spmd.clone.sunk | while | flops 100925440 | bytes 1837663 | solution.py:25
  276.2 1.4 fusion.212
  277.6 1.4 fusion.212
  279.1 1.4 fusion.212
  280.6 1.4 fusion.212
  282.1 1.4 fusion.212
  283.6 1.4 fusion.212
  285.1 1.4 fusion.212
  286.5 1.4 fusion.212
  288.0 1.4 fusion.212
  289.5 1.4 fusion.212
  291.0 1.4 fusion.212
  292.5 1.4 fusion.212
  294.0 1.4 fusion.212
  295.4 1.4 fusion.212
  296.9 1.4 fusion.212
  298.4 1.4 fusion.212
  299.9 1.4 fusion.212
  301.4 1.4 fusion.212
  302.9 1.4 fusion.212
  304.3 1.4 fusion.212
  305.8 1.4 fusion.212
  307.3 1.4 fusion.212
  308.8 1.4 fusion.212
  310.3 1.4 fusion.212
  311.8 1.4 fusion.212
  313.2 1.4 fusion.212
  314.7 1.4 fusion.212
  316.2 1.4 fusion.212
  317.7 1.4 fusion.212
  319.2 1.4 fusion.212
  320.7 1.4 fusion.212
  322.1 61.0 %while.39 = (s32[]{:T(128)}, f32[4,128,128]{2,1,0:T(8,128)S(1)}, f32[2,4,64,128]{3,2,1,0:T(8,128)S(1)}, f32[2,4,64]{2,1,0:T(4,128)}, s32[2,64]{1,0:T(2,128)}, /*...) while((s32[]{:T(128)}, f32[4,128,128]{2,1,0:T(8,128)S(1)}, ...), condition=%wide.region_10.12_spmd, body=%wide.region_9.11_spmd.sunk | while | flops 277717696 | bytes 4313297 | solution.py:262
  322.1 1.2 dynamic_slice.157
  323.4 1.3 fusion.179
  325.5 1.3 fusion.181
  327.6 1.0 fusion.185
  328.6 20.4 %custom-call.11 = f32[4,1,64,64]{2,3,1,0:T(8,128)S(1)} custom-call(f32[4,1,64,64]{3,2,1,0:T(8,128)} %fusion.185), custom_call_target="InvertDiagBlocksLowerTriangular" | custom-call | tf_op jit(solution)/shard_map/while/body/eval_jaxpr/jit(_solve_triangular)/vmap()/triangular_solve | solution.py:90
  352.6 1.2 dynamic_slice.157
  353.9 1.3 fusion.179
  355.9 1.3 fusion.181
  359.1 20.4 %custom-call.11 = f32[4,1,64,64]{2,3,1,0:T(8,128)S(1)} custom-call(f32[4,1,64,64]{3,2,1,0:T(8,128)} %fusion.185), custom_call_target="InvertDiagBlocksLowerTriangular" | custom-call | tf_op jit(solution)/shard_map/while/body/eval_jaxpr/jit(_solve_triangular)/vmap()/triangular_solve | solution.py:90
  383.8 3.5 convolution_convert_fusion
  387.3 30.4 %reduce-scatter.2.cloned.1.call-done = bf16[16,2048]{1,0:T(8,128)(2,1)} async-done(((bf16[128,2048]{1,0:T(8,128)(2,1)}), bf16[16,2048]{1,0:T(8,128)(2,1)}) %reduce-scatter.2.cloned.1.call-update) | async-done | bytes 65552 | tf_op jit(solution)/shard_map/reduce_scatter | solution.py:269
  (194 shorter events, 28.4 us)
Async XLA Ops:
  6.5 377.3 %copy-start = (bf16[512,2048]{1,0:T(8,128)(2,1)S(1)}, bf16[512,2048]{1,0:T(8,128)(2,1)}, u32[]{:S(2)}) copy-start(bf16[512,2048]{1,0:T(8,128)(2,1)} %param.33) | copy-start | bytes 6291460
  6.5 10.4 %copy-start.14 = (s32[16]{0:T(128)S(1)}, s32[16]{0:T(128)}, u32[]{:S(2)}) copy-start(s32[16]{0:T(128)} %param.22) | copy-start | bytes 196
  6.5 11.1 %copy-start.10 = (bf16[4,256]{1,0:T(4,128)(2,1)S(1)}, bf16[4,256]{1,0:T(4,128)(2,1)}, u32[]{:S(2)}) copy-start(bf16[4,256]{1,0:T(4,128)(2,1)} %param.28) | copy-start | bytes 6148
  6.5 11.2 %copy-start.3 = (bf16[4,512]{1,0:T(4,128)(2,1)S(1)}, bf16[4,512]{1,0:T(4,128)(2,1)}, u32[]{:S(2)}) copy-start(bf16[4,512]{1,0:T(4,128)(2,1)} %param.29) | copy-start | bytes 12292
  6.5 12.0 %copy-start.15 = (f32[4]{0:T(128)S(1)}, f32[4]{0:T(128)}, u32[]{:S(2)}) copy-start(f32[4]{0:T(128)} %param.32) | copy-start | bytes 52
  6.5 12.0 %copy-start.12 = (f32[4,128]{1,0:T(4,128)S(1)}, f32[4,128]{1,0:T(4,128)}, u32[]{:S(2)}) copy-start(f32[4,128]{1,0:T(4,128)} %param.30) | copy-start | bytes 6148
  6.6 12.0 %copy-start.13 = (f32[4,128]{1,0:T(4,128)S(1)}, f32[4,128]{1,0:T(4,128)}, u32[]{:S(2)}) copy-start(f32[4,128]{1,0:T(4,128)} %param.31) | copy-start | bytes 6148
  6.6 171.5 %all-gather.5.cloned.1.call-start = ((), (), s32[]{:S(2)}) async-start(), calls=%async_computation.2 | async-start | bytes 8650752 | tf_op jit(solution)/shard_map/all_gather | solution.py:16
  8.5 12.8 %collective-permute-start = (bf16[3,256]{1,0:T(4,128)(2,1)S(1)}, bf16[3,256]{1,0:T(4,128)(2,1)S(1)}, u32[]{:S(2)}, u32[]{:S(2)}) collective-permute-start(bf16[3,256]{1,0:T(4,128)(2,1)S(1)} %slice.206), channel_id=1, source_target_pairs={{0,8},{8,16},{16,24},{24,32},{32,40},{40,48},{48,56},{56,64},{64,7... | collective-permute-start | bytes 4616 | tf_op jit(solution)/shard_map/ppermute | solution.py:31
  13.8 8.2 %collective-permute-start.1 = (bf16[3,512]{1,0:T(4,128)(2,1)S(1)}, bf16[3,512]{1,0:T(4,128)(2,1)S(1)}, u32[]{:S(2)}, u32[]{:S(2)}) collective-permute-start(bf16[3,512]{1,0:T(4,128)(2,1)S(1)} %slice.211), channel_id=1, source_target_pairs={{0,8},{8,16},{16,24},{24,32},{32,40},{40,48},{48,56},{56,64},{64,7... | collective-permute-start | bytes 9224 | tf_op jit(solution)/shard_map/ppermute | solution.py:31
  17.5 4.8 %copy-start.4 = (pred[128]{0:T(512)(128)(4,1)}, pred[128]{0:T(512)(128)(4,1)S(1)}, u32[]{:S(2)}) copy-start(pred[128]{0:T(512)(128)(4,1)S(1)} %get-tuple-element.403) | copy-start | bytes 388
  17.5 4.8 %copy-start.6 = (pred[128]{0:T(512)(128)(4,1)}, pred[128]{0:T(512)(128)(4,1)S(1)}, u32[]{:S(2)}) copy-start(pred[128]{0:T(512)(128)(4,1)S(1)} %get-tuple-element.404) | copy-start | bytes 388
  17.5 4.8 %copy-start.8 = (pred[128]{0:T(512)(128)(4,1)}, pred[128]{0:T(512)(128)(4,1)S(1)}, u32[]{:S(2)}) copy-start(pred[128]{0:T(512)(128)(4,1)S(1)} %get-tuple-element.409) | copy-start | bytes 388
  80.7 0.7 copy-start.1
  80.7 6.1 %copy-start.11 = (bf16[4,256]{1,0:T(4,128)(2,1)S(1)}, bf16[4,256]{1,0:T(4,128)(2,1)}, u32[]{:S(2)}) copy-start(bf16[4,256]{1,0:T(4,128)(2,1)} %param.27) | copy-start | bytes 6148
  80.7 9.7 %copy-start.5 = (pred[128]{0:T(512)(128)(4,1)S(1)}, pred[128]{0:T(512)(128)(4,1)}, u32[]{:S(2)}) copy-start(pred[128]{0:T(512)(128)(4,1)} %copy-done.4) | copy-start | bytes 388
  80.7 9.7 %copy-start.7 = (pred[128]{0:T(512)(128)(4,1)S(1)}, pred[128]{0:T(512)(128)(4,1)}, u32[]{:S(2)}) copy-start(pred[128]{0:T(512)(128)(4,1)} %copy-done.6) | copy-start | bytes 388
  80.7 9.7 %copy-start.9 = (pred[128]{0:T(512)(128)(4,1)S(1)}, pred[128]{0:T(512)(128)(4,1)}, u32[]{:S(2)}) copy-start(pred[128]{0:T(512)(128)(4,1)} %copy-done.8) | copy-start | bytes 388
  81.4 194.7 %all-gather.7.cloned.1.call-start = ((), (), s32[]{:S(2)}) async-start(), calls=%async_computation.3 | async-start | bytes 8650752 | tf_op jit(solution)/shard_map/all_gather | solution.py:16
  82.2 335.5 %reduce-scatter.2.cloned.1.call-start = ((), (), s32[]{:S(2)}) async-start(), calls=%async_computation.1 | async-start | bytes 589824 | tf_op jit(solution)/shard_map/reduce_scatter | solution.py:269
  84.0 6.4 %collective-permute-start.2 = (bf16[3,256]{1,0:T(4,128)(2,1)S(1)}, bf16[3,256]{1,0:T(4,128)(2,1)S(1)}, u32[]{:S(2)}, u32[]{:S(2)}) collective-permute-start(bf16[3,256]{1,0:T(4,128)(2,1)S(1)} %slice.216), channel_id=1, source_target_pairs={{0,8},{8,16},{16,24},{24,32},{32,40},{40,48},{48,56},{56,64},{64,7... | collective-permute-start | bytes 4616 | tf_op jit(solution)/shard_map/ppermute | solution.py:31
  326.8 0.8 copy-start.2
  357.3 0.8 copy-start.2
Sparse Core Ops, SparseCore 0:
  81.6 96.4 all-gather.4
  180.7 95.4 all-gather.6
  387.4 30.2 reduce-scatter.1
where the time goes:
time: 431 us; the launch traced here: 424 us
  waiting for transfers between devices  220 us (51%)
  other arithmetic  95.7 us (22%)
  matrix products  71.7 us (17%)
  between operations  13.6 us (3%)
  local copies, waits for them, and re-layouts  12.8 us (3%)
  starting transfers between devices  9.18 us (2%)
    all_gather x2, waiting for transfers between devices, entering(): pieces = jax.tree.map(lambda part: lax.all_gather(part, axis), value)  185 us
    another operation x16, other arithmetic, stretch_parts(): jax.scipy.linalg.solve_triangular(system, right_side, lower=True, unit_di...  80.5 us
    dot_general x57, matrix products, batched_heads(): return jnp.einsum(form, left_op, right_op, precision=HIGHP)  60.8 us
    reduce_scatter x1, waiting for transfers between devices, per_device(): lax.psum_scatter(jnp.dot(gated_rows, w_output, preferred_element_type=jnp...  30.4 us
    ppermute x3, starting transfers between devices, shifted(): return lax.ppermute(block, axis, route)  9.06 us
  transfers between devices with their start and end apart: 6, of which 4 were waited for; matrix products, arithmetic and copies ran while one was open for 2% of the time, Pallas kernels for 0%

commit v1 on v0

v1 whole, which is shorter than its diff:
```python
import jax
import jax.numpy as jnp
from jax import lax
from jax.experimental import pallas as pl
from jax.experimental.pallas import tpu as pltpu
from jax.sharding import PartitionSpec as P

MESH = pl.DeviceIdType.MESH
F32 = jnp.float32
BF = jnp.bfloat16
T = 128
W = 128
NX = 4
NZ = 8
NY = 4
HV = 4
HK = 2
DOCS = 16
SUB = 16
NCH = 2
D = 2048


def mm(a, b):
    return jnp.dot(a, b, preferred_element_type=F32)


def mm_t(a, b):
    return lax.dot_general(a, b, (((1,), (1,)), ((), ())), preferred_element_type=F32)


def iota(shape, dim):
    return lax.broadcasted_iota(jnp.int32, shape, dim)


def kernel(
    tok_h, doc_h, wq_h, wk_h, wv_h, wg_h, cq_h, ck_h, cv_h, bl_h, dl_h, al_h, wo_h,
    out_ref,
    tok, wq, wk, wv, wg, wo, cq, ck, cv, bl, dl, doc_s, al_s,
    pk, pq, pv, hk, hq, hv, ext, sc8, dm, bdm, dcol, bcol, pick,
    sg, psend, pbuf, o1, qt, qs, rb_mu, rb_u, ssend, srecv, yb, pm, rc, s2, ry,
    lsem, ss, rs_halo, rs_x, rs_z, rs_b, rs_r, rs_c, rs_y,
):
    c = lax.axis_index("ctx")
    hd = lax.axis_index("head")
    z, x = c // NX, c % NX
    y, co = hd // 2, hd % 2

    def at_zx(dz, dx):
        return (lax.rem(z + dz + NZ, NZ) * NX + lax.rem(x + dx, NX), hd)

    def at_y(dy):
        return (c, lax.rem(y + dy, NY) * 2 + co)

    partner = (c, y * 2 + 1 - co)

    def load(i, src, dst):
        cp = pltpu.make_async_copy(src, dst, lsem.at[i])
        cp.start()
        return cp

    l_doc = load(0, doc_h, doc_s)
    l_al = load(1, al_h, al_s)
    l_bl = load(2, bl_h, bl)
    l_dl = load(3, dl_h, dl)
    l_tok = load(4, tok_h, tok)
    l_wk = load(5, wk_h, wk)
    l_wq = load(6, wq_h, wq)
    l_wv = load(7, wv_h, wv)
    l_ck = load(8, ck_h, ck)
    l_cq = load(9, cq_h, cq)
    l_cv = load(10, cv_h, cv)
    l_wg = load(11, wg_h, wg)
    l_wo = load(12, wo_h, wo)

    barrier = pltpu.get_barrier_semaphore()
    sources = [at_zx(0, d) for d in (1, 2, 3)]
    sources += [at_zx(-1, d) for d in range(NX)]
    sources += [at_zx(-3, 0), partner]
    sources += [at_y(d) for d in (1, 2, 3)]
    for dev in sources:
        pl.semaphore_signal(barrier, inc=1, device_id=dev, device_id_type=MESH)

    l_doc.wait()
    l_al.wait()
    l_bl.wait()
    l_dl.wait()
    base = c * T
    offs = []
    total = jnp.int32(0)
    for j in range(DOCS):
        offs.append(total)
        total = total + doc_s[j]
    row = iota((T, T), 0)
    lane = iota((T, T), 1)
    start = jnp.zeros((T, T), jnp.int32)
    start_last = jnp.int32(0)
    for j in range(1, DOCS):
        start = jnp.where(offs[j] <= row + base, offs[j], start)
        start_last = jnp.where(offs[j] <= base + T - 1, offs[j], start_last)
    age = row + base - start
    kept = start < base
    lower = (lane <= row) & (base + lane >= start)
    strict = lane < row
    dlv = dl[...]
    soft = jnp.maximum(dlv, 0.0) + jnp.log(1.0 + jnp.exp(-jnp.abs(dlv)))
    r4 = iota((HV, T), 0)
    rate = jnp.where(r4 == 0, al_s[0], jnp.where(r4 == 1, al_s[1], jnp.where(r4 == 2, al_s[2], al_s[3])))
    sc8[0:HV] = -jnp.exp(rate) * soft
    sc8[HV : 2 * HV] = 1.0 / (1.0 + jnp.exp(-bl[...]))
    both = sc8[...]
    upper = (row <= lane).astype(F32)
    cum = jnp.dot(both, upper, preferred_element_type=F32, precision=lax.Precision.HIGHEST)
    both = jnp.where(iota((2 * HV, T), 0) < HV, cum, both)
    cols = jnp.transpose(both)
    f_row, d_last = [], []
    for h in range(HV):
        gcol = jnp.broadcast_to(cols[:, h : h + 1], (T, T))
        grow = both[h : h + 1, :]
        decay = jnp.exp(jnp.where(lower, gcol - grow, -1e30))
        beta = jnp.broadcast_to(cols[:, HV + h : HV + h + 1], (T, T))
        into = jnp.where(kept, jnp.exp(gcol), 0.0)
        dm[h] = decay
        bdm[h] = jnp.where(strict, decay * beta, 0.0)
        dcol[h] = into
        bcol[h] = beta
        f_row.append(
            jnp.where(
                iota((1, T), 1) + base >= start_last, jnp.exp(gcol[T - 1 : T, :] - grow), 0.0
            )
        )
        d_last.append(into[T - 1 : T, :])
    same_sub = (row >> 4) == (lane >> 4)
    for j in range(SUB - 1):
        pick[:, j * T : (j + 1) * T] = (same_sub & ((row & 15) == j)).astype(F32).astype(BF)

    nxt = (lax.rem(c + 1, NX * NZ), hd)
    sends = []

    def send(i, src, dst, recv, dev):
        cp = pltpu.make_async_remote_copy(
            src_ref=src, dst_ref=dst, send_sem=ss.at[i], recv_sem=recv,
            device_id=dev, device_id_type=MESH,
        )
        cp.start()
        sends.append(cp)
        return cp

    l_tok.wait()
    l_wk.wait()
    pk[...] = mm(tok[...], wk[...]).astype(BF)
    pl.semaphore_wait(barrier, len(sources))
    c_hk = send(0, pk.at[T - 16 : T], hk, rs_halo.at[0], nxt)
    l_wq.wait()
    pq[...] = mm(tok[...], wq[...]).astype(BF)
    c_hq = send(1, pq.at[T - 16 : T], hq, rs_halo.at[1], nxt)
    l_wv.wait()
    pv[...] = mm(tok[...], wv[...]).astype(BF)
    c_hv = send(2, pv.at[T - 16 : T], hv, rs_halo.at[2], nxt)
    l_wg.wait()
    gate = mm(tok[...], wg[...]).astype(BF).astype(F32)
    sg[...] = gate / (1.0 + jnp.exp(-gate))

    ext[8 : 8 + T, 0:256] = pk[...].astype(F32)
    ext[8 : 8 + T, 256:512] = pq[...].astype(F32)
    ext[8 : 8 + T, 512:1024] = pv[...].astype(F32)
    l_ck.wait()
    l_cq.wait()
    l_cv.wait()
    c_hk.wait_recv()
    c_hq.wait_recv()
    c_hv.wait_recv()
    ext[0:8, 0:256] = hk[...].astype(F32)[8:16]
    ext[0:8, 256:512] = hq[...].astype(F32)[8:16]
    ext[0:8, 512:1024] = hv[...].astype(F32)[8:16]

    def conv(first, taps, col):
        wide = slice(first + col, first + col + W)
        w = taps[...].astype(F32)[:, col : col + W]
        acc = w[3:4] * ext[8 : 8 + T, wide]
        for s in (1, 2, 3):
            acc = acc + jnp.where(age >= s, w[3 - s : 4 - s] * ext[8 - s : 8 - s + T, wide], 0.0)
        return acc / (1.0 + jnp.exp(-acc))

    def unit(a):
        return a * lax.rsqrt(jnp.sum(a * a, axis=-1, keepdims=True) + 1e-6)

    keys = [unit(conv(0, ck, n * W)) for n in range(HK)]
    queries = [unit(conv(256, cq, n * W)) * W ** -0.5 for n in range(HK)]
    grams, scores, keys_t = [], [], []
    for n in range(HK):
        kb = keys[n].astype(BF)
        r = mm_t(jnp.concatenate([kb, queries[n].astype(BF)], axis=0), kb)
        grams.append(r[:T])
        scores.append(r[T:])
        keys_t.append(jnp.transpose(keys[n]))
    values = [conv(512, cv, h * W) for h in range(HV)]

    low = [bdm[h] * grams[h // 2] for h in range(HV)]
    packed = []
    lane16 = iota((SUB, T), 1)
    for h in range(HV):
        p = None
        for b in range(T // SUB):
            q = jnp.where((lane16 >> 4) == b, low[h][b * SUB : (b + 1) * SUB], 0.0)
            p = q if p is None else p + q
        packed.append(p)
    coef = mm(jnp.concatenate(packed, axis=0).astype(BF), pick[...])
    inv = [(iota((SUB, T), 0) == (lane16 & 15)).astype(F32) for _ in range(HV)]
    for j in range(SUB - 1):
        for h in range(HV):
            cj = coef[h * SUB : (h + 1) * SUB, j * T : (j + 1) * T]
            inv[h] = inv[h] - cj * inv[h][j : j + 1, :]
    full = [jnp.where(same_sub, jnp.concatenate([inv[h]] * (T // SUB), axis=0), 0.0) for h in range(HV)]
    for shift in (4, 5, 6):
        cut = ((row >> (shift + 1)) == (lane >> (shift + 1))) & ((row >> shift) != (lane >> shift)) & strict
        fb = [full[h].astype(BF) for h in range(HV)]
        m1 = [mm(jnp.where(cut, low[h], 0.0).astype(BF), fb[h]).astype(BF) for h in range(HV)]
        full = [full[h] - mm(fb[h], m1[h]) for h in range(HV)]

    uw = []
    for h in range(HV):
        beta = bcol[h]
        right = jnp.concatenate(
            [(beta * values[h]).astype(BF), (beta * dcol[h] * keys[h // 2]).astype(BF)], axis=1
        )
        uw.append(mm(full[h].astype(BF), right).astype(BF))
    eye = (row == lane).astype(F32)
    for h in range(HV):
        mu = mm((keys_t[h // 2] * f_row[h]).astype(BF), uw[h])
        psend[h] = jnp.concatenate([eye * d_last[h] - mu[:, W:], mu[:, :W]], axis=1).astype(BF)

    c_x = [
        send(2 + d, psend.at[lax.rem(x + d, NX)], pbuf.at[1, x], rs_x.at[d - 1], at_zx(0, d))
        for d in (1, 2, 3)
    ]
    c_z = [
        send(6 + d, psend.at[lax.rem(x + d, NX)], pbuf.at[0, x], rs_z.at[d], at_zx(1, d))
        for d in range(NX)
    ]
    pbuf[1, x] = psend[x]

    for h in range(HV):
        n = h // 2
        oq = mm((dm[h] * scores[n]).astype(BF), uw[h])
        o1[h] = oq[:, :W]
        qt[h] = (dcol[h] * queries[n] - oq[:, W:]).astype(BF)

    for cp in c_x:
        cp.wait_recv()

    def joined(later, earlier):
        r = mm(later[:, :W], earlier)
        return jnp.concatenate([r[:, :W], r[:, W:] + later[:, W:].astype(F32)], axis=1).astype(BF)

    own = [pbuf[1, b] for b in range(NX)]
    c10 = joined(own[1], own[0])
    c32 = joined(own[3], own[2])
    c210 = joined(own[2], c10)
    c3210 = joined(c32, c10)
    for cp in c_z:
        cp.wait_recv()
    prv = [pbuf[0, b] for b in range(NX)]
    p10 = joined(prv[1], prv[0])
    p32 = joined(prv[3], prv[2])
    p3210 = joined(p32, p10)
    two = joined(c3210, p3210)
    qs[0] = two[:, :W]
    qs[1] = two[:, W:]
    c_b1 = send(10, qs, rb_mu, rs_b.at[0], at_zx(1, 0))
    c_b3 = send(11, qs.at[1], rb_u, rs_b.at[1], at_zx(3, 0))
    c_b1.wait_recv()
    c_b3.wait_recv()
    enter = (mm(rb_mu[0], rb_u[...]) + rb_mu[1].astype(F32)).astype(BF)
    ssend[0] = enter
    for b, pair in ((1, own[0]), (2, c10), (3, c210)):
        ssend[b] = (mm(pair[:, :W], enter) + pair[:, W:].astype(F32)).astype(BF)
    c_r = [
        send(11 + d, ssend.at[lax.rem(x + d, NX)], srecv.at[x], rs_r.at[d - 1], at_zx(0, d))
        for d in (1, 2, 3)
    ]
    srecv[x] = ssend[x]
    for cp in c_r:
        cp.wait_recv()

    for h in range(HV):
        o = o1[h] + mm(qt[h], srecv[h])
        o = o * lax.rsqrt(jnp.mean(o * o, axis=-1, keepdims=True) + 1e-6)
        yb[:, h * W : (h + 1) * W] = (o * sg[:, h * W : (h + 1) * W]).astype(BF)
    l_wo.wait()
    cw = D // NCH
    c_c = []
    for n in range(NCH):
        part = mm(yb[...], wo[:, n * cw : (n + 1) * cw]).astype(BF)
        for k in range(2 * NY):
            pm[n, k % 2, k // 2] = part[k * 16 : (k + 1) * 16]
        c_c.append(send(15 + n, pm.at[n, 1 - co], rc.at[n], rs_c.at[n], partner))
    c_y = []
    for n in range(NCH):
        c_c[n].wait_recv()
        s2[n] = (pm[n, co].astype(F32) + rc[n].astype(F32)).astype(BF)
        c_y.append([
            send(15 + NCH + 3 * n + d - 1, s2.at[n, lax.rem(y + d, NY)], ry.at[n, d - 1], rs_y.at[n, d - 1], at_y(d))
            for d in (1, 2, 3)
        ])
    for n in range(NCH):
        for cp in c_y[n]:
            cp.wait_recv()
        tot = pm[n, co, y].astype(F32) + rc[n, y].astype(F32)
        for d in range(3):
            tot = tot + ry[n, d].astype(F32)
        out_ref[:, n * cw : (n + 1) * cw] = tot.astype(BF)
    for cp in sends:
        cp.wait_send()


def per_device(*args):
    vm = pltpu.VMEM
    dma = pltpu.SemaphoreType.DMA
    any_spec = pl.BlockSpec(memory_space=pl.ANY)
    return pl.pallas_call(
        kernel,
        out_shape=jax.ShapeDtypeStruct((16, D), BF),
        in_specs=[any_spec] * 13,
        out_specs=pl.BlockSpec(memory_space=pltpu.VMEM),
        scratch_shapes=[
            vm((T, D), BF), vm((D, 256), BF), vm((D, 256), BF), vm((D, 512), BF), vm((D, 512), BF),
            vm((512, D), BF), vm((4, 256), BF), vm((4, 256), BF), vm((4, 512), BF),
            vm((HV, T), F32), vm((HV, T), F32), pltpu.SMEM((DOCS,), jnp.int32), pltpu.SMEM((HV,), F32),
            vm((T, 256), BF), vm((T, 256), BF), vm((T, 512), BF),
            vm((16, 256), BF), vm((16, 256), BF), vm((16, 512), BF),
            vm((T + 8, 1024), F32), vm((2 * HV, T), F32),
            vm((HV, T, T), F32), vm((HV, T, T), F32), vm((HV, T, T), F32), vm((HV, T, T), F32),
            vm((T, (SUB - 1) * T), BF),
            vm((T, 512), F32),
            vm((HV, W, 2 * W), BF), vm((2, NX, W, 2 * W), BF),
            vm((HV, T, W), F32), vm((HV, T, W), BF),
            vm((2, W, W), BF), vm((2, W, W), BF), vm((W, W), BF),
            vm((NX, W, W), BF), vm((HV, W, W), BF),
            vm((T, 512), BF),
            vm((NCH, 2, NY, 16, D // NCH), BF), vm((NCH, NY, 16, D // NCH), BF),
            vm((NCH, NY, 16, D // NCH), BF), vm((NCH, 3, 16, D // NCH), BF),
            dma((13,)), dma((15 + NCH * 4,)), dma((3,)), dma((3,)), dma((4,)), dma((2,)), dma((3,)),
            dma((NCH,)), dma((NCH, 3)),
        ],
        name="layer",
        compiler_params=pltpu.CompilerParams(
            collective_id=0, has_side_effects=True, vmem_limit_bytes=56 << 20
        ),
    )(*args)


def solution(mesh):
    in_specs = (
        P("ctx", None),
        P(),
        P(None, "head"),
        P(None, "head"),
        P(None, "head"),
        P(None, "head"),
        P(None, "head"),
        P(None, "head"),
        P(None, "head"),
        P("head", "ctx"),
        P("head", "ctx"),
        P("head"),
        P("head", None),
    )
    out_specs = P(("ctx", "head"), None)
    return jax.shard_map(
        per_device, mesh=mesh, in_specs=in_specs, out_specs=out_specs, check_vma=False
    )
```

time: 431 us -> 44.4 us (0.10)
  the two profiles are of different devices: /device:TPU:193 before, /device:TPU:1 now
where the time goes in v1:
time: 44.4 us; the launch traced here: 44.2 us
  Pallas kernels  42.8 us (96%)
  local copies, waits for them, and re-layouts  1.47 us (3%)
    pallas_call x1, Pallas kernels, per_device(): pl.pallas_call(kernel, out_shape=jax.ShapeDtypeStruct((16, D), BF), in_sp...  42.8 us
    unnamed x1, local copies, waits for them, and re-layouts  1.47 us

profile of v1, /device:TPU:1, one launch (start us, length us, event | category | flops | bytes accessed | tf_op | source)
XLA Modules:
  0.0 44.2 jit_solution(18008541208581482759)
XLA Ops:
  0.0 42.8 %layer.1 = bf16[16,2048]{1,0:T(8,128)(2,1)} custom-call(bf16[128,2048]{1,0:T(8,128)(2,1)} %tok_h.1, s32[16]{0:T(128)} %doc_h.1, bf16[2048,256]{1,0:T(8,128)(2,1)} %wq_h.1, bf16[2048,256]{1,0:T(8,128)(2,1)} %wk_h.1, bf16[2048,512]{1,0:T(8,128)(2,1)} %wv_h.1, bf16[2048,512]{1,0:T(8,128)(2,1)} %wg_h.1, bf16[4,256]{1,0:T(4,128)(2,1)} %cq_h.1, ...), custom_call_target="tpu_custom_call" | custom-call | tf_op jit(solution)/shard_map/layer/pallas_call | solution.py:321
  42.8 1.5 %copy.15 = bf16[16,2048]{1,0:T(8,128)(2,1)} copy(bf16[16,2048]{1,0:T(8,128)(2,1)} %layer.1) | data formatting | bytes 131072

commit v2 on v1

--- a/solution.py
+++ b/solution.py
@@ -17,7 +17,7 @@
 HK = 2
 DOCS = 16
 SUB = 16
-NCH = 2
+NCH = 1
 D = 2048
 
 
@@ -65,13 +65,7 @@
     l_dl = load(3, dl_h, dl)
     l_tok = load(4, tok_h, tok)
     l_wk = load(5, wk_h, wk)
-    l_wq = load(6, wq_h, wq)
     l_wv = load(7, wv_h, wv)
-    l_ck = load(8, ck_h, ck)
-    l_cq = load(9, cq_h, cq)
-    l_cv = load(10, cv_h, cv)
-    l_wg = load(11, wg_h, wg)
-    l_wo = load(12, wo_h, wo)
 
     barrier = pltpu.get_barrier_semaphore()
     sources = [at_zx(0, d) for d in (1, 2, 3)]
@@ -80,6 +74,13 @@
     sources += [at_y(d) for d in (1, 2, 3)]
     for dev in sources:
         pl.semaphore_signal(barrier, inc=1, device_id=dev, device_id_type=MESH)
+
+    l_ck = load(8, ck_h, ck)
+    l_cv = load(10, cv_h, cv)
+    l_wq = load(6, wq_h, wq)
+    l_cq = load(9, cq_h, cq)
+    l_wg = load(11, wg_h, wg)
+    l_wo = load(12, wo_h, wo)
 
     l_doc.wait()
     l_al.wait()
@@ -151,28 +152,21 @@
     pk[...] = mm(tok[...], wk[...]).astype(BF)
     pl.semaphore_wait(barrier, len(sources))
     c_hk = send(0, pk.at[T - 16 : T], hk, rs_halo.at[0], nxt)
+    l_wv.wait()
+    pv[...] = mm(tok[...], wv[...]).astype(BF)
+    c_hv = send(2, pv.at[T - 16 : T], hv, rs_halo.at[2], nxt)
     l_wq.wait()
     pq[...] = mm(tok[...], wq[...]).astype(BF)
     c_hq = send(1, pq.at[T - 16 : T], hq, rs_halo.at[1], nxt)
-    l_wv.wait()
-    pv[...] = mm(tok[...], wv[...]).astype(BF)
-    c_hv = send(2, pv.at[T - 16 : T], hv, rs_halo.at[2], nxt)
     l_wg.wait()
-    gate = mm(tok[...], wg[...]).astype(BF).astype(F32)
-    sg[...] = gate / (1.0 + jnp.exp(-gate))
+    sg[...] = mm(tok[...], wg[...]).astype(BF).astype(F32)
 
     ext[8 : 8 + T, 0:256] = pk[...].astype(F32)
     ext[8 : 8 + T, 256:512] = pq[...].astype(F32)
     ext[8 : 8 + T, 512:1024] = pv[...].astype(F32)
     l_ck.wait()
+    l_cv.wait()
     l_cq.wait()
-    l_cv.wait()
-    c_hk.wait_recv()
-    c_hq.wait_recv()
-    c_hv.wait_recv()
-    ext[0:8, 0:256] = hk[...].astype(F32)[8:16]
-    ext[0:8, 256:512] = hq[...].astype(F32)[8:16]
-    ext[0:8, 512:1024] = hv[...].astype(F32)[8:16]
 
     def conv(first, taps, col):
         wide = slice(first + col, first + col + W)
@@ -185,15 +179,14 @@
     def unit(a):
         return a * lax.rsqrt(jnp.sum(a * a, axis=-1, keepdims=True) + 1e-6)
 
+    c_hk.wait_recv()
+    ext[0:8, 0:256] = hk[...].astype(F32)[8:16]
     keys = [unit(conv(0, ck, n * W)) for n in range(HK)]
-    queries = [unit(conv(256, cq, n * W)) * W ** -0.5 for n in range(HK)]
-    grams, scores, keys_t = [], [], []
-    for n in range(HK):
-        kb = keys[n].astype(BF)
-        r = mm_t(jnp.concatenate([kb, queries[n].astype(BF)], axis=0), kb)
-        grams.append(r[:T])
-        scores.append(r[T:])
-        keys_t.append(jnp.transpose(keys[n]))
+    keys_b = [k.astype(BF) for k in keys]
+    keys_t = [jnp.transpose(k) for k in keys]
+    grams = [mm_t(k, k) for k in keys_b]
+    c_hv.wait_recv()
+    ext[0:8, 512:1024] = hv[...].astype(F32)[8:16]
     values = [conv(512, cv, h * W) for h in range(HV)]
 
     low = [bdm[h] * grams[h // 2] for h in range(HV)]
@@ -230,16 +223,22 @@
         mu = mm((keys_t[h // 2] * f_row[h]).astype(BF), uw[h])
         psend[h] = jnp.concatenate([eye * d_last[h] - mu[:, W:], mu[:, :W]], axis=1).astype(BF)
 
+    c_z = [
+        send(6 + d, psend.at[lax.rem(x + d, NX)], pbuf.at[0, x], rs_z.at[d], at_zx(1, d))
+        for d in range(NX)
+    ]
     c_x = [
         send(2 + d, psend.at[lax.rem(x + d, NX)], pbuf.at[1, x], rs_x.at[d - 1], at_zx(0, d))
         for d in (1, 2, 3)
     ]
-    c_z = [
-        send(6 + d, psend.at[lax.rem(x + d, NX)], pbuf.at[0, x], rs_z.at[d], at_zx(1, d))
-        for d in range(NX)
-    ]
     pbuf[1, x] = psend[x]
 
+    c_hq.wait_recv()
+    ext[0:8, 256:512] = hq[...].astype(F32)[8:16]
+    queries = [unit(conv(256, cq, n * W)) * W ** -0.5 for n in range(HK)]
+    scores = [mm_t(queries[n].astype(BF), keys_b[n]) for n in range(HK)]
+    gate = sg[...]
+    sg[...] = gate / (1.0 + jnp.exp(-gate))
     for h in range(HV):
         n = h // 2
         oq = mm((dm[h] * scores[n]).astype(BF), uw[h])
@@ -267,8 +266,8 @@
     two = joined(c3210, p3210)
     qs[0] = two[:, :W]
     qs[1] = two[:, W:]
+    c_b3 = send(11, qs.at[1], rb_u, rs_b.at[1], at_zx(3, 0))
     c_b1 = send(10, qs, rb_mu, rs_b.at[0], at_zx(1, 0))
-    c_b3 = send(11, qs.at[1], rb_u, rs_b.at[1], at_zx(3, 0))
     c_b1.wait_recv()
     c_b3.wait_recv()
     enter = (mm(rb_mu[0], rb_u[...]) + rb_mu[1].astype(F32)).astype(BF)
@@ -320,7 +319,7 @@
     any_spec = pl.BlockSpec(memory_space=pl.ANY)
     return pl.pallas_call(
         kernel,
-        out_shape=jax.ShapeDtypeStruct((16, D), BF),
+        out_shape=pltpu.VMEM((16, D), BF),
         in_specs=[any_spec] * 13,
         out_specs=pl.BlockSpec(memory_space=pltpu.VMEM),
         scratch_shapes=[

time: 44.4 us -> 41.2 us (0.928)
  Pallas kernels: 42.8 us -> 40.5 us
  local copies, waits for them, and re-layouts: 1.47 us -> 0.63 us
    pallas_call x1, Pallas kernels: 42.8 us -> 40.5 us  [per_device(): pl.pallas_call(kernel, out_shape=pltpu.VMEM((16, D), BF), in_specs=[any_s...]
    unnamed x1, local copies, waits for them, and re-layouts: 1.47 us -> 0.63 us
where the time goes in v2:
time: 41.2 us; the launch traced here: 41.1 us
  Pallas kernels  40.5 us (98%)
  local copies, waits for them, and re-layouts  0.63 us (2%)
    pallas_call x1, Pallas kernels, per_device(): pl.pallas_call(kernel, out_shape=pltpu.VMEM((16, D), BF), in_specs=[any_s...  40.5 us

profile of v2, /device:TPU:1, one launch (start us, length us, event | category | flops | bytes accessed | tf_op | source)
XLA Modules:
  0.0 41.1 jit_solution(16220423797804836601)
XLA Ops:
  0.0 40.5 %layer.1 = bf16[16,2048]{1,0:T(8,128)(2,1)S(1)} custom-call(bf16[128,2048]{1,0:T(8,128)(2,1)} %tok_h.1, s32[16]{0:T(128)} %doc_h.1, bf16[2048,256]{1,0:T(8,128)(2,1)} %wq_h.1, bf16[2048,256]{1,0:T(8,128)(2,1)} %wk_h.1, bf16[2048,512]{1,0:T(8,128)(2,1)} %wv_h.1, bf16[2048,512]{1,0:T(8,128)(2,1)} %wg_h.1, bf16[4,256]{1,0:T(4,128)(2,1)} %cq_h.1, ...), custom_call_target="tpu_custom_call" | custom-call | tf_op jit(solution)/shard_map/layer/pallas_call | solution.py:320
  40.5 0.6 %copy.15 = bf16[16,2048]{1,0:T(8,128)(2,1)} copy(bf16[16,2048]{1,0:T(8,128)(2,1)S(1)} %layer.1) | data formatting | bytes 131072

commit v3 on v2

--- a/solution.py
+++ b/solution.py
@@ -39,7 +39,7 @@
     tok, wq, wk, wv, wg, wo, cq, ck, cv, bl, dl, doc_s, al_s,
     pk, pq, pv, hk, hq, hv, ext, sc8, dm, bdm, dcol, bcol, pick,
     sg, psend, pbuf, o1, qt, qs, rb_mu, rb_u, ssend, srecv, yb, pm, rc, s2, ry,
-    lsem, ss, rs_halo, rs_x, rs_z, rs_b, rs_r, rs_c, rs_y,
+    ready_h, ready_1, ready_3, lsem, ss, rs_halo, rs_x, rs_z, rs_b, rs_r, rs_c, rs_y,
 ):
     c = lax.axis_index("ctx")
     hd = lax.axis_index("head")
@@ -68,12 +68,22 @@
     l_wv = load(7, wv_h, wv)
 
     barrier = pltpu.get_barrier_semaphore()
-    sources = [at_zx(0, d) for d in (1, 2, 3)]
-    sources += [at_zx(-1, d) for d in range(NX)]
-    sources += [at_zx(-3, 0), partner]
-    sources += [at_y(d) for d in (1, 2, 3)]
-    for dev in sources:
-        pl.semaphore_signal(barrier, inc=1, device_id=dev, device_id_type=MESH)
+
+    def hello(sem, dev):
+        pl.semaphore_signal(sem, inc=1, device_id=dev, device_id_type=MESH)
+
+    mates = [at_zx(0, d) for d in (1, 2, 3)] + [partner] + [at_y(d) for d in (1, 2, 3)]
+    for dev in mates:
+        hello(barrier, dev)
+
+    @pl.when(z < NZ - 1)
+    def _():
+        for d in range(NX):
+            hello(barrier, at_zx(1, d))
+
+    @pl.when(z < NZ - 3)
+    def _():
+        hello(barrier, at_zx(3, 0))
 
     l_ck = load(8, ck_h, ck)
     l_cv = load(10, cv_h, cv)
@@ -135,29 +145,80 @@
     for j in range(SUB - 1):
         pick[:, j * T : (j + 1) * T] = (same_sub & ((row & 15) == j)).astype(F32).astype(BF)
 
+    @pl.when(c == 0)
+    def _():
+        hk[...] = jnp.zeros_like(hk)
+        hq[...] = jnp.zeros_like(hq)
+        hv[...] = jnp.zeros_like(hv)
+
+    @pl.when(z == 0)
+    def _():
+        pbuf[0] = jnp.zeros((NX, W, 2 * W), BF)
+        rb_mu[...] = jnp.zeros_like(rb_mu)
+
+    @pl.when(z < 3)
+    def _():
+        rb_u[...] = jnp.zeros_like(rb_u)
+
+    earlier = jnp.where(z > 0, NX, 0) + jnp.where(z > 2, 1, 0)
+    pl.semaphore_wait(barrier, len(mates) + earlier)
+
+    @pl.when(z > 0)
+    def _():
+        for d in range(NX):
+            hello(ready_1.at[(NX - d) % NX], at_zx(-1, d))
+
+    @pl.when((z > 0) & (x == 0))
+    def _():
+        hello(ready_h, at_zx(-1, NX - 1))
+
+    @pl.when(z > 2)
+    def _():
+        hello(ready_3, at_zx(-3, 0))
+
     nxt = (lax.rem(c + 1, NX * NZ), hd)
     sends = []
 
-    def send(i, src, dst, recv, dev):
-        cp = pltpu.make_async_remote_copy(
+    def copy(i, src, dst, recv, dev):
+        return pltpu.make_async_remote_copy(
             src_ref=src, dst_ref=dst, send_sem=ss.at[i], recv_sem=recv,
             device_id=dev, device_id_type=MESH,
         )
+
+    def send(i, src, dst, recv, dev):
+        cp = copy(i, src, dst, recv, dev)
         cp.start()
-        sends.append(cp)
+        sends.append((None, cp))
         return cp
 
+    def send_if(cond, cp):
+        @pl.when(cond)
+        def _():
+            cp.start()
+
+    c_hk = copy(0, pk.at[T - 16 : T], hk, rs_halo.at[0], nxt)
+    c_hq = copy(1, pq.at[T - 16 : T], hq, rs_halo.at[1], nxt)
+    c_hv = copy(2, pv.at[T - 16 : T], hv, rs_halo.at[2], nxt)
+    sends += [(c < NX * NZ - 1, cp) for cp in (c_hk, c_hq, c_hv)]
+    inner = x < NX - 1
     l_tok.wait()
     l_wk.wait()
     pk[...] = mm(tok[...], wk[...]).astype(BF)
-    pl.semaphore_wait(barrier, len(sources))
-    c_hk = send(0, pk.at[T - 16 : T], hk, rs_halo.at[0], nxt)
+    send_if(inner, c_hk)
     l_wv.wait()
     pv[...] = mm(tok[...], wv[...]).astype(BF)
-    c_hv = send(2, pv.at[T - 16 : T], hv, rs_halo.at[2], nxt)
+    send_if(inner, c_hv)
     l_wq.wait()
     pq[...] = mm(tok[...], wq[...]).astype(BF)
-    c_hq = send(1, pq.at[T - 16 : T], hq, rs_halo.at[1], nxt)
+    send_if(inner, c_hq)
+
+    @pl.when((x == NX - 1) & (z < NZ - 1))
+    def _():
+        pl.semaphore_wait(ready_h, 1)
+        c_hk.start()
+        c_hv.start()
+        c_hq.start()
+
     l_wg.wait()
     sg[...] = mm(tok[...], wg[...]).astype(BF).astype(F32)
 
@@ -179,13 +240,21 @@
     def unit(a):
         return a * lax.rsqrt(jnp.sum(a * a, axis=-1, keepdims=True) + 1e-6)
 
-    c_hk.wait_recv()
+
+    @pl.when(c > 0)
+    def _():
+        c_hk.wait_recv()
+
     ext[0:8, 0:256] = hk[...].astype(F32)[8:16]
     keys = [unit(conv(0, ck, n * W)) for n in range(HK)]
     keys_b = [k.astype(BF) for k in keys]
     keys_t = [jnp.transpose(k) for k in keys]
     grams = [mm_t(k, k) for k in keys_b]
-    c_hv.wait_recv()
+
+    @pl.when(c > 0)
+    def _():
+        c_hv.wait_recv()
+
     ext[0:8, 512:1024] = hv[...].astype(F32)[8:16]
     values = [conv(512, cv, h * W) for h in range(HV)]
 
@@ -223,17 +292,29 @@
         mu = mm((keys_t[h // 2] * f_row[h]).astype(BF), uw[h])
         psend[h] = jnp.concatenate([eye * d_last[h] - mu[:, W:], mu[:, :W]], axis=1).astype(BF)
 
-    c_z = [
-        send(6 + d, psend.at[lax.rem(x + d, NX)], pbuf.at[0, x], rs_z.at[d], at_zx(1, d))
-        for d in range(NX)
-    ]
     c_x = [
         send(2 + d, psend.at[lax.rem(x + d, NX)], pbuf.at[1, x], rs_x.at[d - 1], at_zx(0, d))
         for d in (1, 2, 3)
     ]
+    c_z = [
+        copy(6 + d, psend.at[lax.rem(x + d, NX)], pbuf.at[0, x], rs_z.at[d], at_zx(1, d))
+        for d in range(NX)
+    ]
+    sends += [(z < NZ - 1, cp) for cp in c_z]
+
+    @pl.when(z < NZ - 1)
+    def _():
+        for d in range(NX):
+            pl.semaphore_wait(ready_1.at[d], 1)
+            c_z[d].start()
+
     pbuf[1, x] = psend[x]
 
-    c_hq.wait_recv()
+
+    @pl.when(c > 0)
+    def _():
+        c_hq.wait_recv()
+
     ext[0:8, 256:512] = hq[...].astype(F32)[8:16]
     queries = [unit(conv(256, cq, n * W)) * W ** -0.5 for n in range(HK)]
     scores = [mm_t(queries[n].astype(BF), keys_b[n]) for n in range(HK)]
@@ -257,8 +338,12 @@
     c32 = joined(own[3], own[2])
     c210 = joined(own[2], c10)
     c3210 = joined(c32, c10)
-    for cp in c_z:
-        cp.wait_recv()
+
+    @pl.when(z > 0)
+    def _():
+        for cp in c_z:
+            cp.wait_recv()
+
     prv = [pbuf[0, b] for b in range(NX)]
     p10 = joined(prv[1], prv[0])
     p32 = joined(prv[3], prv[2])
@@ -266,10 +351,25 @@
     two = joined(c3210, p3210)
     qs[0] = two[:, :W]
     qs[1] = two[:, W:]
-    c_b3 = send(11, qs.at[1], rb_u, rs_b.at[1], at_zx(3, 0))
-    c_b1 = send(10, qs, rb_mu, rs_b.at[0], at_zx(1, 0))
-    c_b1.wait_recv()
-    c_b3.wait_recv()
+    c_b3 = copy(11, qs.at[1], rb_u, rs_b.at[1], at_zx(3, 0))
+    c_b1 = copy(10, qs, rb_mu, rs_b.at[0], at_zx(1, 0))
+    sends += [(z < NZ - 3, c_b3), (z < NZ - 1, c_b1)]
+
+    @pl.when(z < NZ - 3)
+    def _():
+        pl.semaphore_wait(ready_3, 1)
+        c_b3.start()
+
+    send_if(z < NZ - 1, c_b1)
+
+    @pl.when(z > 0)
+    def _():
+        c_b1.wait_recv()
+
+    @pl.when(z > 2)
+    def _():
+        c_b3.wait_recv()
+
     enter = (mm(rb_mu[0], rb_u[...]) + rb_mu[1].astype(F32)).astype(BF)
     ssend[0] = enter
     for b, pair in ((1, own[0]), (2, c10), (3, c210)):
@@ -309,8 +409,11 @@
         for d in range(3):
             tot = tot + ry[n, d].astype(F32)
         out_ref[:, n * cw : (n + 1) * cw] = tot.astype(BF)
-    for cp in sends:
-        cp.wait_send()
+    for cond, cp in sends:
+        if cond is None:
+            cp.wait_send()
+        else:
+            pl.when(cond)(cp.wait_send)
 
 
 def per_device(*args):
@@ -339,6 +442,7 @@
             vm((T, 512), BF),
             vm((NCH, 2, NY, 16, D // NCH), BF), vm((NCH, NY, 16, D // NCH), BF),
             vm((NCH, NY, 16, D // NCH), BF), vm((NCH, 3, 16, D // NCH), BF),
+            pltpu.SemaphoreType.REGULAR, pltpu.SemaphoreType.REGULAR((NX,)), pltpu.SemaphoreType.REGULAR,
             dma((13,)), dma((15 + NCH * 4,)), dma((3,)), dma((3,)), dma((4,)), dma((2,)), dma((3,)),
             dma((NCH,)), dma((NCH, 3)),
         ],

time: 41.2 us -> 38.3 us (0.930)
  the two profiles are of different devices: /device:TPU:1 before, /device:TPU:193 now
where the time goes in v3:
time: 38.3 us; the launch traced here: 38.2 us
  Pallas kernels  37.6 us (98%)
  local copies, waits for them, and re-layouts  0.63 us (2%)
    pallas_call x1, Pallas kernels, per_device(): pl.pallas_call(kernel, out_shape=pltpu.VMEM((16, D), BF), in_specs=[any_s...  37.6 us

profile of v3, /device:TPU:193, one launch (start us, length us, event | category | flops | bytes accessed | tf_op | source)
XLA Modules:
  0.0 38.2 jit_solution(17133025166825066270)
XLA Ops:
  0.0 37.6 %layer.1 = bf16[16,2048]{1,0:T(8,128)(2,1)S(1)} custom-call(bf16[128,2048]{1,0:T(8,128)(2,1)} %tok_h.1, s32[16]{0:T(128)} %doc_h.1, bf16[2048,256]{1,0:T(8,128)(2,1)} %wq_h.1, bf16[2048,256]{1,0:T(8,128)(2,1)} %wk_h.1, bf16[2048,512]{1,0:T(8,128)(2,1)} %wv_h.1, bf16[2048,512]{1,0:T(8,128)(2,1)} %wg_h.1, bf16[4,256]{1,0:T(4,128)(2,1)} %cq_h.1, ...), custom_call_target="tpu_custom_call" | custom-call | tf_op jit(solution)/shard_map/layer/pallas_call | solution.py:423
  37.6 0.6 %copy.15 = bf16[16,2048]{1,0:T(8,128)(2,1)} copy(bf16[16,2048]{1,0:T(8,128)(2,1)S(1)} %layer.1) | data formatting | bytes 131072

commit v4 on v3

--- a/solution.py
+++ b/solution.py
@@ -39,7 +39,7 @@
     tok, wq, wk, wv, wg, wo, cq, ck, cv, bl, dl, doc_s, al_s,
     pk, pq, pv, hk, hq, hv, ext, sc8, dm, bdm, dcol, bcol, pick,
     sg, psend, pbuf, o1, qt, qs, rb_mu, rb_u, ssend, srecv, yb, pm, rc, s2, ry,
-    ready_h, ready_1, ready_3, lsem, ss, rs_halo, rs_x, rs_z, rs_b, rs_r, rs_c, rs_y,
+    ready_1, ready_3, lsem, ss, rs_halo, rs_x, rs_z, rs_b, rs_r, rs_c, rs_y,
 ):
     c = lax.axis_index("ctx")
     hd = lax.axis_index("head")
@@ -75,6 +75,10 @@
     mates = [at_zx(0, d) for d in (1, 2, 3)] + [partner] + [at_y(d) for d in (1, 2, 3)]
     for dev in mates:
         hello(barrier, dev)
+
+    @pl.when((z > 0) & (x == 0))
+    def _():
+        hello(barrier, at_zx(-1, NX - 1))
 
     @pl.when(z < NZ - 1)
     def _():
@@ -160,22 +164,6 @@
     def _():
         rb_u[...] = jnp.zeros_like(rb_u)
 
-    earlier = jnp.where(z > 0, NX, 0) + jnp.where(z > 2, 1, 0)
-    pl.semaphore_wait(barrier, len(mates) + earlier)
-
-    @pl.when(z > 0)
-    def _():
-        for d in range(NX):
-            hello(ready_1.at[(NX - d) % NX], at_zx(-1, d))
-
-    @pl.when((z > 0) & (x == 0))
-    def _():
-        hello(ready_h, at_zx(-1, NX - 1))
-
-    @pl.when(z > 2)
-    def _():
-        hello(ready_3, at_zx(-3, 0))
-
     nxt = (lax.rem(c + 1, NX * NZ), hd)
     sends = []
 
@@ -200,24 +188,31 @@
     c_hq = copy(1, pq.at[T - 16 : T], hq, rs_halo.at[1], nxt)
     c_hv = copy(2, pv.at[T - 16 : T], hv, rs_halo.at[2], nxt)
     sends += [(c < NX * NZ - 1, cp) for cp in (c_hk, c_hq, c_hv)]
-    inner = x < NX - 1
+    more = c < NX * NZ - 1
     l_tok.wait()
     l_wk.wait()
     pk[...] = mm(tok[...], wk[...]).astype(BF)
-    send_if(inner, c_hk)
+
+    earlier = jnp.where(z > 0, NX, 0) + jnp.where(z > 2, 1, 0)
+    after = jnp.where((z < NZ - 1) & (x == NX - 1), 1, 0)
+    pl.semaphore_wait(barrier, len(mates) + earlier + after)
+
+    @pl.when(z > 0)
+    def _():
+        for d in range(NX):
+            hello(ready_1.at[(NX - d) % NX], at_zx(-1, d))
+
+    @pl.when(z > 2)
+    def _():
+        hello(ready_3, at_zx(-3, 0))
+
+    send_if(more, c_hk)
     l_wv.wait()
     pv[...] = mm(tok[...], wv[...]).astype(BF)
-    send_if(inner, c_hv)
+    send_if(more, c_hv)
     l_wq.wait()
     pq[...] = mm(tok[...], wq[...]).astype(BF)
-    send_if(inner, c_hq)
-
-    @pl.when((x == NX - 1) & (z < NZ - 1))
-    def _():
-        pl.semaphore_wait(ready_h, 1)
-        c_hk.start()
-        c_hv.start()
-        c_hq.start()
+    send_if(more, c_hq)
 
     l_wg.wait()
     sg[...] = mm(tok[...], wg[...]).astype(BF).astype(F32)
@@ -442,7 +437,7 @@
             vm((T, 512), BF),
             vm((NCH, 2, NY, 16, D // NCH), BF), vm((NCH, NY, 16, D // NCH), BF),
             vm((NCH, NY, 16, D // NCH), BF), vm((NCH, 3, 16, D // NCH), BF),
-            pltpu.SemaphoreType.REGULAR, pltpu.SemaphoreType.REGULAR((NX,)), pltpu.SemaphoreType.REGULAR,
+            pltpu.SemaphoreType.REGULAR((NX,)), pltpu.SemaphoreType.REGULAR,
             dma((13,)), dma((15 + NCH * 4,)), dma((3,)), dma((3,)), dma((4,)), dma((2,)), dma((3,)),
             dma((NCH,)), dma((NCH, 3)),
         ],

time: 38.3 us -> 34.6 us (0.903)
  Pallas kernels: 37.6 us -> 33.9 us
    pallas_call x1, Pallas kernels: 37.6 us -> 33.9 us  [per_device(): pl.pallas_call(kernel, out_shape=pltpu.VMEM((16, D), BF), in_specs=[any_s...]
where the time goes in v4:
time: 34.6 us; the launch traced here: 34.5 us
  Pallas kernels  33.9 us (98%)
  local copies, waits for them, and re-layouts  0.63 us (2%)
    pallas_call x1, Pallas kernels, per_device(): pl.pallas_call(kernel, out_shape=pltpu.VMEM((16, D), BF), in_specs=[any_s...  33.9 us

profile of v4, /device:TPU:193, one launch (start us, length us, event | category | flops | bytes accessed | tf_op | source)
XLA Modules:
  0.0 34.5 jit_solution(17418789111455817412)
XLA Ops:
  0.0 33.9 %layer.1 = bf16[16,2048]{1,0:T(8,128)(2,1)S(1)} custom-call(bf16[128,2048]{1,0:T(8,128)(2,1)} %tok_h.1, s32[16]{0:T(128)} %doc_h.1, bf16[2048,256]{1,0:T(8,128)(2,1)} %wq_h.1, bf16[2048,256]{1,0:T(8,128)(2,1)} %wk_h.1, bf16[2048,512]{1,0:T(8,128)(2,1)} %wv_h.1, bf16[2048,512]{1,0:T(8,128)(2,1)} %wg_h.1, bf16[4,256]{1,0:T(4,128)(2,1)} %cq_h.1, ...), custom_call_target="tpu_custom_call" | custom-call | tf_op jit(solution)/shard_map/layer/pallas_call | solution.py:418
  33.9 0.6 %copy.15 = bf16[16,2048]{1,0:T(8,128)(2,1)} copy(bf16[16,2048]{1,0:T(8,128)(2,1)S(1)} %layer.1) | data formatting | bytes 131072

commit v5 on v4

--- a/solution.py
+++ b/solution.py
@@ -343,22 +343,27 @@
     p10 = joined(prv[1], prv[0])
     p32 = joined(prv[3], prv[2])
     p3210 = joined(p32, p10)
-    two = joined(c3210, p3210)
-    qs[0] = two[:, :W]
-    qs[1] = two[:, W:]
+    qs[1] = (mm(c3210[:, :W], p3210[:, W:]) + c3210[:, W:].astype(F32)).astype(BF)
     c_b3 = copy(11, qs.at[1], rb_u, rs_b.at[1], at_zx(3, 0))
-    c_b1 = copy(10, qs, rb_mu, rs_b.at[0], at_zx(1, 0))
-    sends += [(z < NZ - 3, c_b3), (z < NZ - 1, c_b1)]
+    c_b1 = copy(10, qs.at[1], rb_mu.at[1], rs_b.at[0], at_zx(1, 0))
+    c_b0 = copy(15 + 4 * NCH, qs.at[0], rb_mu.at[0], rs_b.at[2], at_zx(1, 0))
+    sends += [(z < NZ - 3, c_b3), (z < NZ - 1, c_b1), (z < NZ - 1, c_b0)]
 
     @pl.when(z < NZ - 3)
     def _():
         pl.semaphore_wait(ready_3, 1)
         c_b3.start()
 
-    send_if(z < NZ - 1, c_b1)
+    qs[0] = mm(c3210[:, :W], p3210[:, :W]).astype(BF)
+
+    @pl.when(z < NZ - 1)
+    def _():
+        c_b0.start()
+        c_b1.start()
 
     @pl.when(z > 0)
     def _():
+        c_b0.wait_recv()
         c_b1.wait_recv()
 
     @pl.when(z > 2)
@@ -438,7 +443,7 @@
             vm((NCH, 2, NY, 16, D // NCH), BF), vm((NCH, NY, 16, D // NCH), BF),
             vm((NCH, NY, 16, D // NCH), BF), vm((NCH, 3, 16, D // NCH), BF),
             pltpu.SemaphoreType.REGULAR((NX,)), pltpu.SemaphoreType.REGULAR,
-            dma((13,)), dma((15 + NCH * 4,)), dma((3,)), dma((3,)), dma((4,)), dma((2,)), dma((3,)),
+            dma((13,)), dma((16 + NCH * 4,)), dma((3,)), dma((3,)), dma((4,)), dma((3,)), dma((3,)),
             dma((NCH,)), dma((NCH, 3)),
         ],
         name="layer",

time: 34.6 us -> 34.7 us (level)
  no operation moved by 1% of the time
where the time goes in v5:
time: 34.7 us; the launch traced here: 34.6 us
  Pallas kernels  33.9 us (98%)
  local copies, waits for them, and re-layouts  0.63 us (2%)
    pallas_call x1, Pallas kernels, per_device(): pl.pallas_call(kernel, out_shape=pltpu.VMEM((16, D), BF), in_specs=[any_s...  33.9 us

profile of v5, /device:TPU:193, one launch (start us, length us, event | category | flops | bytes accessed | tf_op | source)
XLA Modules:
  0.0 34.6 jit_solution(10144029599250111217)
XLA Ops:
  0.0 33.9 %layer.1 = bf16[16,2048]{1,0:T(8,128)(2,1)S(1)} custom-call(bf16[128,2048]{1,0:T(8,128)(2,1)} %tok_h.1, s32[16]{0:T(128)} %doc_h.1, bf16[2048,256]{1,0:T(8,128)(2,1)} %wq_h.1, bf16[2048,256]{1,0:T(8,128)(2,1)} %wk_h.1, bf16[2048,512]{1,0:T(8,128)(2,1)} %wv_h.1, bf16[2048,512]{1,0:T(8,128)(2,1)} %wg_h.1, bf16[4,256]{1,0:T(4,128)(2,1)} %cq_h.1, ...), custom_call_target="tpu_custom_call" | custom-call | tf_op jit(solution)/shard_map/layer/pallas_call | solution.py:423
  34.0 0.6 %copy.15 = bf16[16,2048]{1,0:T(8,128)(2,1)} copy(bf16[16,2048]{1,0:T(8,128)(2,1)S(1)} %layer.1) | data formatting | bytes 131072
